TPU v7x, 32 devices: a whole 2x2x4 slice. The times are simulated.
32 devices in a mesh: sub: 8 (over z, y), ifc: 4 (over x, core).
Axes of the slice: x: 2, y: 2, z: 4, core: 2. Of those that a mesh axis runs over, the one named last changes fastest.
Arguments:
- gap: float32 [8, 1024, 128], P('sub', 'ifc'), may hold values from -6 to 6
- flexibility: float32 [8, 2, 1024, 2048], P('sub', None, 'ifc'), may hold values from -1 to 4, as said below
- stiffness: float32 [8, 2, 1024, 2048], P('sub', None, 'ifc'), may hold values from -1 to 4, as said below
- modes: float32 [8, 6, 2, 1024], P('sub', None, None, 'ifc'), may hold values from -1 to 1
- mode_counts: int32 [8], P('sub'), may hold values from 3 to 6
Outputs:
- multipliers: float32 [8, 1024, 128], P('sub', 'ifc')
- residual: float32 [8, 1024, 128], P('sub', 'ifc')
Inputs may be any that keep to these rules, and one draw needn't show every extreme that they name: `flexibility`: each subdomain's block, as a matrix of order 2 * 1024, is symmetric positive definite. `stiffness`: each subdomain's block, as a matrix of order 2 * 1024, is symmetric positive definite.
All inputs are finite; a program needn't handle non-finite values.
Results may differ from a plain program's by a relative error of at most 0.0003.
Values sent between devices are 32-bit elements; how exact they have to be, the bound alone decides.
A program may use at most 64 MiB of HBM per device.

v0:
```python
import jax
import jax.numpy as jnp
from jax import lax
from jax.sharding import PartitionSpec as P

precise = lax.Precision.HIGHEST


def shifted_2(block, axis, distance):
    devices = range(lax.axis_size(axis))
    route = [(i - distance, i) for i in devices if i - distance in devices]
    return lax.ppermute(block, axis, route)


def assemble(own_blocks, next_blocks, off_blocks):
    subs_count = own_blocks.shape[0]
    mode_count = own_blocks.shape[1]
    shifted = jnp.concatenate(
        [jnp.zeros((1, mode_count, mode_count), jnp.float32), next_blocks[:-1]], 0
    )
    diag_blocks = own_blocks + shifted
    ident = jnp.eye(subs_count, dtype=jnp.float32)
    upper = jnp.eye(subs_count, k=1, dtype=jnp.float32)
    whole = jnp.einsum("st,sij->sitj", ident, diag_blocks, precision=precise)
    whole = whole + jnp.einsum("st,sij->sitj", upper, off_blocks, precision=precise)
    whole = whole + jnp.einsum("st,sij->tjsi", upper, off_blocks, precision=precise)
    return whole.reshape(subs_count * mode_count, subs_count * mode_count)


def coarse_solve(factor, rhs_matrix):
    forward = lax.linalg.triangular_solve(factor, rhs_matrix, left_side=True, lower=True)
    return lax.linalg.triangular_solve(
        factor, forward, left_side=True, lower=True, transpose_a=True
    )


def apply_jump(matrix, vector, edge_live):
    own_rows = vector.shape[0]
    face_len = own_rows * lax.axis_size("ifc")
    block_rows = matrix[0].reshape(2, own_rows, 2, face_len)
    whole_face = lax.all_gather(vector, "ifc", axis=0, tiled=True)
    before = shifted_2(whole_face, "sub", 1)
    traces = jnp.stack([-before, whole_face], 0)
    image = jnp.einsum("aibj,bjk->aik", block_rows, traces, precision=precise)
    after = shifted_2(image[0], "sub", -1)
    return (image[1] - after) * edge_live


def inner(first_vec, second_vec):
    return lax.psum(jnp.sum(first_vec * second_vec, axis=0), ("sub", "ifc"))


def per_device(gap, flexibility, stiffness, modes, mode_counts):
    subs_count = lax.axis_size("sub")
    lanes = lax.axis_size("ifc")
    sub_index = lax.axis_index("sub")
    edge_live = (sub_index < subs_count - 1).astype(jnp.float32)
    first_lane = (lax.axis_index("ifc") == 0).astype(jnp.float32)
    mode_count = modes.shape[1]
    load_count = gap.shape[2]
    active = (jnp.arange(mode_count) < mode_counts[0]).astype(jnp.float32)
    mode_right = modes[0, :, 1] * active[:, None] * edge_live
    mode_next = shifted_2(modes[0, :, 0] * active[:, None], "sub", -1)
    own_blocks = jnp.dot(mode_right, mode_right.T, precision=precise)
    own_blocks = (
        own_blocks + jnp.eye(mode_count, dtype=jnp.float32) * (1.0 - active)[:, None] * first_lane
    )
    next_blocks = jnp.dot(mode_next, mode_next.T, precision=precise)
    off_blocks = -jnp.dot(mode_right, mode_next.T, precision=precise)
    partial_blocks = jnp.stack([own_blocks, next_blocks, off_blocks], 0)
    gathered = lax.all_gather(partial_blocks[None], ("sub", "ifc"), axis=0, tiled=True)
    gathered = gathered.reshape(subs_count, lanes, 3, mode_count, mode_count).sum(1)
    factor = jnp.linalg.cholesky(assemble(gathered[:, 0], gathered[:, 1], gathered[:, 2]))

    def project(vector):
        own_part = jnp.dot(mode_right, vector, precision=precise)
        next_part = -jnp.dot(mode_next, vector, precision=precise)
        partial_terms = jnp.stack([own_part, next_part], 0)
        joined = lax.all_gather(partial_terms[None], ("sub", "ifc"), axis=0, tiled=True)
        all_partials = joined.reshape(subs_count, lanes, 2, mode_count, load_count).sum(1)
        coarse_rhs = all_partials[:, 0] + jnp.concatenate(
            [jnp.zeros((1, mode_count, load_count), jnp.float32), all_partials[:-1, 1]], 0
        )
        weights = coarse_solve(
            factor, coarse_rhs.reshape(subs_count * mode_count, load_count)
        ).reshape(subs_count, mode_count, load_count)
        weight_own = lax.dynamic_index_in_dim(weights, sub_index, 0, keepdims=False)
        weight_next = lax.dynamic_index_in_dim(
            weights, jnp.minimum(sub_index + 1, subs_count - 1), 0, keepdims=False
        )
        correction = jnp.dot(mode_right.T, weight_own, precision=precise) - jnp.dot(
            mode_next.T, weight_next, precision=precise
        )
        return vector - correction

    residual = project(gap[0] * edge_live)
    search = project(0.25 * apply_jump(stiffness, residual, edge_live))
    rz_now = inner(residual, search)
    image = project(apply_jump(flexibility, search, edge_live))
    step_size = rz_now / inner(search, image)
    multipliers = step_size * search
    residual = residual - step_size * image
    return (multipliers[None], residual[None])


def solution(mesh):
    return jax.shard_map(
        per_device,
        mesh=mesh,
        in_specs=(
            P("sub", "ifc", None),
            P("sub", None, "ifc", None),
            P("sub", None, "ifc", None),
            P("sub", None, None, "ifc"),
            P("sub"),
        ),
        out_specs=(P("sub", "ifc", None), P("sub", "ifc", None)),
        check_vma=False,
    )
```

profile of v0, /device:TPU:0, one launch (start us, length us, event | category | flops | bytes accessed | tf_op | source)
XLA Modules:
  0.0 287.8 jit_solution(17114196268054613221)
XLA Ops:
  1.3 0.8 fusion.107
  2.2 1.3 collective-permute-start
  3.5 1.1 convolution_bitcast_fusion.2
  4.7 0.2 fusion.17
  4.9 3.8 %collective-permute-done = f32[6,256]{1,0:T(8,128)S(1)} collective-permute-done((f32[6,256]{1,0:T(8,128)S(1)}, f32[6,256]{1,0:T(8,128)S(1)}, u32[]{:S(2)}, u32[]{:S(2)}) %collective-permute-start) | collective-permute-done | bytes 6176 | tf_op jit(solution)/shard_map/ppermute | solution.py:12
  8.7 0.2 fusion.16
  9.0 41.6 %all-gather = f32[96,6,6]{2,1,0:T(8,128)S(1)} all-gather(f32[3,6,6]{2,1,0:T(8,128)S(1)} %pad_maximum_fusion), channel_id=2, replica_groups=mesh['sub'=8,'ifc'=4] {'sub','ifc'}, dimensions={0}, use_global_device_ids=true | all-gather | bytes 14256 | tf_op jit(solution)/shard_map/all_gather | solution.py:71
  51.1 0.5 copy.34
  51.9 4.4 %cholesky.18 = f32[48,48]{1,0:T(8,128)S(1)} custom-call(f32[48,48]{1,0:T(8,128)S(1)} %fusion.52), custom_call_target="Cholesky" | custom-call | tf_op jit(solution)/shard_map/jit(cholesky)/cholesky | solution.py:73
  56.4 0.6 compare_reduce_fusion
  57.0 0.7 fusion.39
  57.7 3.7 %custom-call.14 = f32[1,48,48]{1,2,0:T(8,128)S(1)} custom-call(f32[1,48,48]{2,1,0:T(8,128)S(1)} %fusion.39), custom_call_target="InvertDiagBlocksLowerTriangular" | custom-call | tf_op jit(solution)/shard_map/triangular_solve/custom-call.2 | solution.py:32
  61.3 1.1 fusion.15
  62.4 37.4 %all-gather.1 = f32[64,6,128]{2,1,0:T(8,128)S(1)} all-gather(f32[2,6,128]{2,1,0:T(8,128)S(1)} %pad_maximum_fusion.1), channel_id=3, replica_groups=mesh['sub'=8,'ifc'=4] {'sub','ifc'}, dimensions={0}, use_global_device_ids=true | all-gather | bytes 202752 | tf_op jit(solution)/shard_map/all_gather | solution.py:79
  99.9 0.2 fusion.48
  100.1 0.1 fusion.50
  100.3 0.5 fusion.65
  100.7 0.4 fusion.12
  101.1 7.4 %all_gather.20 = f32[1024,128]{1,0:T(8,128)S(1)} all-gather(f32[256,128]{1,0:T(8,128)S(1)} %fusion.12), channel_id=1, replica_groups=mesh['sub'=8,'ifc'=4] {'ifc'}, dimensions={0}, use_global_device_ids=true | all-gather | bytes 655360 | tf_op jit(solution)/shard_map/all_gather | solution.py:41
  108.5 1.3 collective-permute-start.1
  109.8 6.6 %reshape_squeeze.6 = f32[2,256,2,1024]{3,2,1,0:T(2,128)} reshape(f32[1,2,256,2048]{3,2,1,0:T(8,128)} %param.11) | data formatting | bytes 8388608 | tf_op jit(solution)/shard_map/reshape;squeeze | solution.py:40
  116.4 5.3 %collective-permute-done.1 = f32[1024,128]{1,0:T(8,128)S(1)} collective-permute-done((f32[1024,128]{1,0:T(8,128)S(1)}, f32[1024,128]{1,0:T(8,128)S(1)}, u32[]{:S(2)}, u32[]{:S(2)}) %collective-permute-start.1) | collective-permute-done | bytes 524320 | tf_op jit(solution)/shard_map/ppermute | solution.py:12
  121.8 6.2 %fusion.4 = f32[2,256,128]{2,1,0:T(8,128)S(1)} fusion(f32[2,256,2,1024]{3,2,1,0:T(2,128)} %reshape_squeeze.6, f32[1,1024,128]{2,1,0:T(8,128)S(1)} %bitcast.207, f32[1,1024,128]{2,1,0:T(8,128)S(1)} %negate_bitcast_fusion.1), kind=kOutput, calls=%fused_computation.4 | convolution fusion | flops 1610874880 | bytes 5505024 | tf_op jit(solution)/shard_map/aibj,bjk->aik/dot_general | solution.py:44
  128.0 1.3 collective-permute-start.2
  129.3 6.5 %collective-permute-done.2 = f32[256,128]{1,0:T(8,128)S(1)} collective-permute-done((f32[256,128]{1,0:T(8,128)S(1)}, f32[256,128]{1,0:T(8,128)S(1)}, u32[]{:S(2)}, u32[]{:S(2)}) %collective-permute-start.2) | collective-permute-done | bytes 131104 | tf_op jit(solution)/shard_map/ppermute | solution.py:12
  135.8 0.2 convolution_bitcast_fusion.1
  136.1 0.2 fusion.14
  136.3 38.6 %all-gather.2 = f32[64,6,128]{2,1,0:T(8,128)S(1)} all-gather(f32[2,6,128]{2,1,0:T(8,128)S(1)} %pad_maximum_fusion.2), channel_id=4, replica_groups=mesh['sub'=8,'ifc'=4] {'sub','ifc'}, dimensions={0}, use_global_device_ids=true | all-gather | bytes 202752 | tf_op jit(solution)/shard_map/all_gather | solution.py:79
  175.0 0.2 fusion.44
  175.2 0.1 fusion.46
  175.4 0.5 fusion.63
  175.8 0.4 fusion.11
  176.2 7.3 %all_gather.22 = f32[1024,128]{1,0:T(8,128)S(1)} all-gather(f32[256,128]{1,0:T(8,128)S(1)} %fusion.11), channel_id=1, replica_groups=mesh['sub'=8,'ifc'=4] {'ifc'}, dimensions={0}, use_global_device_ids=true | all-gather | bytes 655360 | tf_op jit(solution)/shard_map/all_gather | solution.py:41
  183.5 1.5 collective-permute-start.3
  185.0 6.6 %reshape_squeeze.7 = f32[2,256,2,1024]{3,2,1,0:T(2,128)} reshape(f32[1,2,256,2048]{3,2,1,0:T(8,128)} %param.10) | data formatting | bytes 8388608 | tf_op jit(solution)/shard_map/reshape;squeeze | solution.py:40
  191.6 5.2 %collective-permute-done.3 = f32[1024,128]{1,0:T(8,128)S(1)} collective-permute-done((f32[1024,128]{1,0:T(8,128)S(1)}, f32[1024,128]{1,0:T(8,128)S(1)}, u32[]{:S(2)}, u32[]{:S(2)}) %collective-permute-start.3) | collective-permute-done | bytes 524320 | tf_op jit(solution)/shard_map/ppermute | solution.py:12
  196.8 6.2 %fusion.7 = f32[2,256,128]{2,1,0:T(8,128)S(1)} fusion(f32[2,256,2,1024]{3,2,1,0:T(2,128)} %reshape_squeeze.7, f32[1,1024,128]{2,1,0:T(8,128)S(1)} %bitcast.208, f32[1,1024,128]{2,1,0:T(8,128)S(1)} %negate_bitcast_fusion), kind=kOutput, calls=%fused_computation.5 | convolution fusion | flops 1610874880 | bytes 5505024 | tf_op jit(solution)/shard_map/aibj,bjk->aik/dot_general | solution.py:44
  203.0 1.3 collective-permute-start.4
  204.3 6.5 %collective-permute-done.4 = f32[256,128]{1,0:T(8,128)S(1)} collective-permute-done((f32[256,128]{1,0:T(8,128)S(1)}, f32[256,128]{1,0:T(8,128)S(1)}, u32[]{:S(2)}, u32[]{:S(2)}) %collective-permute-start.4) | collective-permute-done | bytes 131104 | tf_op jit(solution)/shard_map/ppermute | solution.py:12
  210.8 0.2 convolution_bitcast_fusion
  211.1 0.2 fusion.13
  211.3 37.5 %all-gather.3 = f32[64,6,128]{2,1,0:T(8,128)S(1)} all-gather(f32[2,6,128]{2,1,0:T(8,128)S(1)} %pad_maximum_fusion.3), channel_id=5, replica_groups=mesh['sub'=8,'ifc'=4] {'sub','ifc'}, dimensions={0}, use_global_device_ids=true | all-gather | bytes 202752 | tf_op jit(solution)/shard_map/all_gather | solution.py:79
  248.8 0.2 fusion.40
  249.1 0.1 fusion.42
  249.2 0.5 fusion.61
  249.7 0.4 multiply_reduce_fusion
  250.1 36.9 %all-reduce.4 = (f32[128]{0:T(128)S(1)}, f32[128]{0:T(128)S(1)}) all-reduce(f32[128]{0:T(128)S(1)} %get-tuple-element.5, f32[128]{0:T(128)S(1)} %get-tuple-element.4), channel_id=1, replica_groups=mesh['sub'=8,'ifc'=4] {'sub','ifc'}, use_global_device_ids=true, to_apply=%region_6.0 | all-reduce | flops 256 | bytes 2048 | tf_op jit(solution)/shard_map/psum | solution.py:50
  287.0 0.7 subtract_bitcast_fusion
  (46 shorter events, 1.3 us)
Async XLA Ops:
  0.6 100.1 %copy-start = (f32[1,256,128]{2,1,0:T(8,128)S(1)}, f32[1,256,128]{2,1,0:T(8,128)}, u32[]{:S(2)}) copy-start(f32[1,256,128]{2,1,0:T(8,128)} %param.9) | copy-start | bytes 393220
  2.2 6.5 %collective-permute-start = (f32[6,256]{1,0:T(8,128)S(1)}, f32[6,256]{1,0:T(8,128)S(1)}, u32[]{:S(2)}, u32[]{:S(2)}) collective-permute-start(f32[6,256]{1,0:T(8,128)S(1)} %fusion.57), channel_id=1, source_target_pairs={{4,0},{8,4},{12,8},{16,12},{20,16},{24,20},{28,24},{5,1},{9,5},{13... | collective-permute-start | bytes 18440 | tf_op jit(solution)/shard_map/ppermute | solution.py:12
  108.5 13.2 %collective-permute-start.1 = (f32[1024,128]{1,0:T(8,128)S(1)}, f32[1024,128]{1,0:T(8,128)S(1)}, u32[]{:S(2)}, u32[]{:S(2)}) collective-permute-start(f32[1024,128]{1,0:T(8,128)S(1)} %all_gather.20), channel_id=1, source_target_pairs={{0,4},{4,8},{8,12},{12,16},{16,20},{20,24},{24,28},{1,5},{5,9},{9,... | collective-permute-start | bytes 1572872 | tf_op jit(solution)/shard_map/ppermute | solution.py:12
  128.0 7.8 %collective-permute-start.2 = (f32[256,128]{1,0:T(8,128)S(1)}, f32[256,128]{1,0:T(8,128)S(1)}, u32[]{:S(2)}, u32[]{:S(2)}) collective-permute-start(f32[256,128]{1,0:T(8,128)S(1)} %slice_bitcast_fusion.2), channel_id=1, source_target_pairs={{4,0},{8,4},{12,8},{16,12},{20,16},{24,20},{28,24},{5,1},{9,5},{13... | collective-permute-start | bytes 393224 | tf_op jit(solution)/shard_map/ppermute | solution.py:12
  183.5 13.2 %collective-permute-start.3 = (f32[1024,128]{1,0:T(8,128)S(1)}, f32[1024,128]{1,0:T(8,128)S(1)}, u32[]{:S(2)}, u32[]{:S(2)}) collective-permute-start(f32[1024,128]{1,0:T(8,128)S(1)} %all_gather.22), channel_id=1, source_target_pairs={{0,4},{4,8},{8,12},{12,16},{16,20},{20,24},{24,28},{1,5},{5,9},{9,... | collective-permute-start | bytes 1572872 | tf_op jit(solution)/shard_map/ppermute | solution.py:12
  203.0 7.8 %collective-permute-start.4 = (f32[256,128]{1,0:T(8,128)S(1)}, f32[256,128]{1,0:T(8,128)S(1)}, u32[]{:S(2)}, u32[]{:S(2)}) collective-permute-start(f32[256,128]{1,0:T(8,128)S(1)} %slice_bitcast_fusion), channel_id=1, source_target_pairs={{4,0},{8,4},{12,8},{16,12},{20,16},{24,20},{28,24},{5,1},{9,5},{13... | collective-permute-start | bytes 393224 | tf_op jit(solution)/shard_map/ppermute | solution.py:12
where the time goes:
time: 289 us; the launch traced here: 288 us
  blocking collectives  207 us (72%)
  waiting for transfers between devices  27.4 us (9%)
  matrix products  19.6 us (7%)
  local copies, waits for them, and re-layouts  15 us (5%)
  other arithmetic  10.7 us (4%)
  starting transfers between devices  6.67 us (2%)
    all_gather x3, blocking collectives, project(): lax.all_gather(partial_terms[None], ('sub', 'ifc'), axis=0, tiled=True)  113 us
    all_gather x1, blocking collectives, per_device(): lax.all_gather(partial_blocks[None], ('sub', 'ifc'), axis=0, tiled=True)  41.6 us
    psum x1, blocking collectives, inner(): return lax.psum(jnp.sum(first_vec * second_vec, axis=0), ('sub', 'ifc'))  36.9 us
    ppermute x5, waiting for transfers between devices, shifted_2(): return lax.ppermute(block, axis, route)  27.4 us
    all_gather x2, blocking collectives, apply_jump(): whole_face = lax.all_gather(vector, 'ifc', axis=0, tiled=True)  14.6 us
    another operation x2, local copies, waits for them, and re-layouts, apply_jump(): block_rows = matrix[0].reshape(2, own_rows, 2, face_len)  13.2 us
    dot_general x2, matrix products, apply_jump(): image = jnp.einsum('aibj,bjk->aik', block_rows, traces, precision=precise)  12.4 us
    ppermute x5, starting transfers between devices, shifted_2(): return lax.ppermute(block, axis, route)  6.67 us
  transfers between devices with their start and end apart: 5, of which 5 were waited for; matrix products, arithmetic and copies ran while one was open for 5% of the time, Pallas kernels for 0%

commit v1 on v0

v1 whole, which is shorter than its diff:
```python
import functools

import jax
import jax.numpy as jnp
from jax import lax
from jax.experimental import pallas as pl
from jax.experimental.pallas import tpu as pltpu
from jax.sharding import PartitionSpec as P

MESH = pl.DeviceIdType.MESH
precise = lax.Precision.HIGHEST
f32 = jnp.float32


def dot_nn(a, b):
    return lax.dot_general(a, b, (((1,), (0,)), ((), ())), precision=precise, preferred_element_type=f32)


def dot_nt(a, b):
    return lax.dot_general(a, b, (((1,), (1,)), ((), ())), precision=precise, preferred_element_type=f32)


def dot_tn(a, b):
    return lax.dot_general(a, b, (((0,), (0,)), ((), ())), precision=precise, preferred_element_type=f32)


def split(a):
    hi = a.astype(jnp.bfloat16)
    lo = (a - hi.astype(f32)).astype(jnp.bfloat16)
    return hi, lo


def kernel(S, L, R, gap_ref, k_hbm, f_hbm, modes_ref, mult_ref, res_ref,
           k_v, f_v, nbm, mt, t_buf, nbg, u_buf, nbu, v_buf, nbv, part, red, wbuf, own, acc,
           load_sem, nb_send, nb_recv, ag_send, ag_recv, mt_send, mt_recv,
           ln_send, ln_recv, sb_send, sb_recv):
    X = L // 2
    n = 8 * S
    nw = -(-n // 128) * 128
    s = lax.axis_index("sub")
    lane = lax.axis_index("ifc")
    x, core = lane // 2, lane % 2
    mate = x * 2 + (1 - core)
    has_l, has_r = s > 0, s < S - 1
    m_l, m_r = has_l.astype(f32), has_r.astype(f32)
    left, right = jnp.maximum(s - 1, 0), jnp.minimum(s + 1, S - 1)

    loads = [pltpu.make_async_copy(k_hbm, k_v, load_sem.at[0]),
             pltpu.make_async_copy(f_hbm, f_v, load_sem.at[1])]
    for load in loads:
        load.start()

    def rc(src, dst, ss, rs, sub, ln):
        return pltpu.make_async_remote_copy(src_ref=src, dst_ref=dst, send_sem=ss, recv_sem=rs,
                                            device_id=(sub, ln), device_id_type=MESH)

    barrier = pltpu.get_barrier_semaphore()
    for d in range(1, L):
        pl.semaphore_signal(barrier, inc=1, device_id=(s, lax.rem(lane + d, L)), device_id_type=MESH)
    for d in range(1, S):
        pl.semaphore_signal(barrier, inc=1, device_id=(lax.rem(s + d, S), lane), device_id_type=MESH)

    t_buf[0, 1, lane] = gap_ref[...] * m_r

    @pl.when(jnp.logical_not(has_l))
    def _():
        nbm[0] = jnp.zeros_like(nbm[0])
        nbg[...] = jnp.zeros_like(nbg)
        nbu[0] = jnp.zeros_like(nbu[0])

    @pl.when(jnp.logical_not(has_r))
    def _():
        nbm[1] = jnp.zeros_like(nbm[1])
        nbu[1] = jnp.zeros_like(nbu[1])
        nbv[...] = jnp.zeros_like(nbv)

    pl.semaphore_wait(barrier, (L - 1) + (S - 1))

    to_left = {
        0: rc(modes_ref.at[pl.ds(0, 16)], nbm.at[1], nb_send.at[0], nb_recv.at[0], left, lane),
        3: rc(u_buf.at[0], nbu.at[1], nb_send.at[3], nb_recv.at[3], left, lane),
        5: rc(v_buf, nbv, nb_send.at[5], nb_recv.at[5], left, lane),
    }
    to_right = {
        1: rc(modes_ref.at[pl.ds(0, 16)], nbm.at[0], nb_send.at[1], nb_recv.at[1], right, lane),
        2: rc(t_buf.at[0, 1, lane], nbg, nb_send.at[2], nb_recv.at[2], right, lane),
        4: rc(u_buf.at[1], nbu.at[0], nb_send.at[4], nb_recv.at[4], right, lane),
    }

    def nb_start(which):
        copy, cond = (to_left[which], has_l) if which in to_left else (to_right[which], has_r)

        @pl.when(cond)
        def _():
            copy.start()

    def nb_wait(which):
        copy, cond = (to_left[which], has_r) if which in to_left else (to_right[which], has_l)

        @pl.when(cond)
        def _():
            copy.wait_recv()

    sends = []

    def ag_copy(r, f, src, slot, dst):
        piece = t_buf.at[r, f, src]
        return rc(piece, piece, ag_send.at[r, f, slot], ag_recv.at[r, f, src], s, dst)

    def ag_start(r, f):
        for d in range(1, X):
            copy = ag_copy(r, f, lane, d, lax.rem(x + d, X) * 2 + core)
            copy.start()
            sends.append(copy)
        copy = ag_copy(r, f, lane, 0, mate)
        copy.start()
        sends.append(copy)

    def ag_forward(r, f):
        for d in range(1, X):
            src = lax.rem(x + d, X) * 2 + core
            copy = ag_copy(r, f, src, X - 1 + d, mate)
            copy.wait_recv()
            copy.start()
            sends.append(copy)

    def lane_send(r, rows):
        for d in range(1, L):
            block = part.at[r, lane, pl.ds(0, rows)]
            copy = rc(block, block, ln_send.at[r, d], ln_recv.at[r, lane], s, lax.rem(lane + d, L))
            copy.start()
            sends.append(copy)

    def lane_sum(r, rows):
        total = part[r, lane, 0:rows]
        for d in range(1, L):
            src = lax.rem(lane + d, L)
            block = part.at[r, src, pl.ds(0, rows)]
            rc(block, block, ln_send.at[r, d], ln_recv.at[r, src], s, src).wait_recv()
            total = total + part[r, src, 0:rows]
        return total

    def sub_send(r, rows, value):
        red[r, s, 0:rows] = value
        block = red.at[r, s, pl.ds(0, rows)]
        for d in range(1, S):
            copy = rc(block, block, sb_send.at[r, d], sb_recv.at[r, s], lax.rem(s + d, S), lane)
            copy.start()
            sends.append(copy)

    def sub_wait(r, rows):
        for d in range(1, S):
            src = lax.rem(s + d, S)
            block = red.at[r, src, pl.ds(0, rows)]
            rc(block, block, sb_send.at[r, d], sb_recv.at[r, src], src, lane).wait_recv()

    def rhs_of(r):
        rows = []
        for t in range(S):
            row = red[r, t, 8:16]
            if t > 0:
                row = row + red[r, t - 1, 16:24]
            if t < S - 1:
                row = row + red[r, t + 1, 0:8]
            rows.append(row)
        return jnp.concatenate(rows, 0)

    def inner_of(r):
        total = red[r, 0, 24:25]
        for t in range(1, S):
            total = total + red[r, t, 24:25]
        return total

    def weights_of(r, inverse):
        wbuf[r, 0:8] = jnp.zeros((8, 128), f32)
        wbuf[r, n + 8:n + 16] = jnp.zeros((8, 128), f32)
        wbuf[r, 8:n + 8] = dot_nn(inverse, rhs_of(r))
        return wbuf[r, pl.ds(pl.multiple_of(s * 8, 8), 24)]

    nb_start(0)
    nb_start(1)
    ag_start(0, 1)
    nb_start(2)
    nb_wait(0)
    nb_wait(1)
    modes_left, modes_right = modes_ref[0:8], modes_ref[8:16]
    zero = jnp.zeros((8, R), f32)
    mt_l = jnp.concatenate([-nbm[0, 8:16], modes_left * m_l, zero], 0)
    mt_r = jnp.concatenate([zero, modes_right, -nbm[1, 0:8]], 0)
    mt[lane, 0] = mt_l
    mt[lane, 1] = mt_r
    gram = dot_nt(mt_l[8:16], mt_l) + dot_nt(mt_r[8:16], mt_r)
    part[0, lane, 0:24] = dot_nn(mt_r, t_buf[0, 1, lane])
    part[0, lane, 24:32] = jnp.concatenate([gram, jnp.zeros((8, 104), f32)], 1)
    lane_send(0, 32)
    for d in range(1, L):
        copy = rc(mt.at[lane], mt.at[lane], mt_send.at[d], mt_recv.at[lane], s, lax.rem(lane + d, L))
        copy.start()
        sends.append(copy)
    nb_wait(2)
    t_buf[0, 0, lane] = -nbg[...]
    ag_start(0, 0)
    total = lane_sum(0, 32)
    idle = jnp.where(
        lax.broadcasted_iota(jnp.int32, (8, 128), 0) + 8 == lax.broadcasted_iota(jnp.int32, (8, 128), 1),
        modes_ref[16:24, 0:128], 0.0)
    sub_send(0, 32, jnp.concatenate([total[0:24], total[24:32] + idle], 0))
    ag_forward(0, 1)
    sub_wait(0, 32)

    rows = []
    for t in range(S):
        row = red[0, t, 24:32]
        if nw > 128:
            row = jnp.concatenate([row, jnp.zeros((8, nw - 128), f32)], 1)
        rows.append(pltpu.roll(row, (8 * (t - 1)) % nw, 1) if t != 1 else row)
    coarse = jnp.concatenate(rows, 0)
    row_at = lax.broadcasted_iota(jnp.int32, (n, nw), 0)
    col_at = lax.broadcasted_iota(jnp.int32, (n, nw), 1)

    def sweep(a, k, row):
        col = jnp.sum(jnp.where(col_at == k, a, 0.0), axis=1, keepdims=True)
        pivot = jnp.sum(jnp.where(col_at[0:1] == k, row, 0.0), axis=1, keepdims=True)
        scale = 1.0 / pivot
        scaled = jnp.where(col_at[0:1] == k, -scale, row * scale)
        base = jnp.where(col_at == k, 0.0, a)
        col = jnp.where(row_at[:, 0:1] == k, -1.0, col)
        return jnp.where(row_at == k, scaled, base - col * jnp.where(col_at[0:1] == k, -scale, row * scale))

    if n <= 64:
        for t in range(S):
            for m in range(6):
                k = 8 * t + m
                coarse = sweep(coarse, k, coarse[k:k + 1])
    else:
        def step(i, a):
            k = 8 * (i // 6) + lax.rem(i, 6)
            return sweep(a, k, jnp.sum(jnp.where(row_at == k, a, 0.0), axis=0, keepdims=True))
        coarse = lax.fori_loop(0, 6 * S, step, coarse)
    pad = lax.rem(row_at, 8) >= 6
    inverse = jnp.where(pad, jnp.where(row_at == col_at, 1.0, 0.0), -coarse)[:, 0:n]

    ag_forward(0, 0)
    for d in range(1, L):
        src = lax.rem(lane + d, L)
        rc(mt.at[src], mt.at[src], mt_send.at[d], mt_recv.at[src], s, src).wait_recv()

    def multiply(r, matrix, weights):
        acc[...] = jnp.zeros_like(acc)
        order = [(lane, False), (mate, True)]
        order += [(lax.rem(x + d, X) * 2 + core, False) for d in range(1, X)]
        order += [(lax.rem(x + d, X) * 2 + 1 - core, True) for d in range(1, X)]
        for j, wait in order:
            for f in (1, 0):
                if wait:
                    ag_copy(r, f, j, 0, mate).wait_recv()
                piece = t_buf[r, f, j] - dot_tn(mt[j, f], weights)
                if j is lane:
                    own[r, f] = piece
                columns = pl.ds(pl.multiple_of(f * (L * R) + j * R, R), R)
                p_hi, p_lo = split(piece)
                for h in range(2):
                    m_hi, m_lo = split(matrix[h, :, columns])
                    acc[h] += (
                        jnp.dot(m_hi, p_hi, preferred_element_type=f32)
                        + jnp.dot(m_hi, p_lo, preferred_element_type=f32)
                        + jnp.dot(m_lo, p_hi, preferred_element_type=f32)
                    )

    weights = weights_of(0, inverse)
    loads[0].wait()
    multiply(0, k_v, weights)

    u_buf[0] = acc[0] * 0.25
    u_buf[1] = acc[1] * 0.25
    nb_start(3)
    nb_start(4)
    dots = jnp.sum(own[0, 0] * u_buf[0] + own[0, 1] * u_buf[1], axis=0, keepdims=True)
    part[1, lane, 0:24] = dot_nn(mt_l, u_buf[0]) + dot_nn(mt_r, u_buf[1])
    part[1, lane, 24:32] = jnp.broadcast_to(dots, (8, 128))
    lane_send(1, 32)
    nb_wait(3)
    t_buf[1, 1, lane] = (u_buf[1] - nbu[1]) * m_r
    ag_start(1, 1)
    nb_wait(4)
    t_buf[1, 0, lane] = (u_buf[0] - nbu[0]) * m_l
    ag_start(1, 0)
    sub_send(1, 32, lane_sum(1, 32))
    ag_forward(1, 1)
    ag_forward(1, 0)
    sub_wait(1, 32)
    weights = weights_of(1, inverse)
    loads[1].wait()
    multiply(1, f_v, weights)

    v_buf[...] = acc[0]
    nb_start(5)
    dots = jnp.sum(own[1, 0] * acc[0] + own[1, 1] * acc[1], axis=0, keepdims=True)
    part[2, lane, 0:24] = dot_nn(mt_l, acc[0]) + dot_nn(mt_r, acc[1])
    part[2, lane, 24:32] = jnp.broadcast_to(dots, (8, 128))
    lane_send(2, 32)
    sub_send(2, 32, lane_sum(2, 32))
    nb_wait(5)
    image = (acc[1] - nbv[...]) * m_r
    sub_wait(2, 32)
    step_size = inner_of(1) / inner_of(2)
    image = image - dot_tn(mt_r, weights_of(2, inverse))
    mult_ref[...] = step_size * own[1, 1]
    res_ref[...] = own[0, 1] - step_size * image

    for copy in sends:
        copy.wait_send()

    @pl.when(has_l)
    def _():
        for copy in to_left.values():
            copy.wait_send()

    @pl.when(has_r)
    def _():
        for copy in to_right.values():
            copy.wait_send()


def per_device(gap, flexibility, stiffness, modes, mode_counts):
    S, L = lax.axis_size("sub"), lax.axis_size("ifc")
    R, n = gap.shape[1], 8 * lax.axis_size("sub")
    count, loads = modes.shape[1], gap.shape[2]
    live = (lax.axis_index("sub") < S - 1).astype(f32)
    active = (jnp.arange(8) < mode_counts[0]).astype(f32)
    faces = jnp.pad(jnp.swapaxes(modes[0], 0, 1), ((0, 0), (0, 8 - count), (0, 0)))
    faces = faces * active[None, :, None]
    idle = jnp.broadcast_to(1.0 - active[:, None], (8, R))
    packed = jnp.concatenate([faces[0], faces[1] * live, idle], 0)
    vm = pl.BlockSpec(memory_space=pltpu.VMEM)
    hbm = pl.BlockSpec(memory_space=pl.ANY)
    dma = pltpu.SemaphoreType.DMA
    mult, res = pl.pallas_call(
        functools.partial(kernel, S, L, R),
        out_shape=[jax.ShapeDtypeStruct((R, loads), f32)] * 2,
        in_specs=[vm, hbm, hbm, vm],
        out_specs=[vm, vm],
        scratch_shapes=[
            pltpu.VMEM((2, R, 2 * L * R), f32),
            pltpu.VMEM((2, R, 2 * L * R), f32),
            pltpu.VMEM((2, 16, R), f32),
            pltpu.VMEM((L, 2, 24, R), f32),
            pltpu.VMEM((2, 2, L, R, loads), f32),
            pltpu.VMEM((R, loads), f32),
            pltpu.VMEM((2, R, loads), f32),
            pltpu.VMEM((2, R, loads), f32),
            pltpu.VMEM((R, loads), f32),
            pltpu.VMEM((R, loads), f32),
            pltpu.VMEM((3, L, 32, 128), f32),
            pltpu.VMEM((3, S, 32, 128), f32),
            pltpu.VMEM((3, n + 16, 128), f32),
            pltpu.VMEM((2, 2, R, loads), f32),
            pltpu.VMEM((2, R, loads), f32),
            dma((2,)),
            dma((6,)),
            dma((6,)),
            dma((2, 2, L)),
            dma((2, 2, L)),
            dma((L,)),
            dma((L,)),
            dma((3, L)),
            dma((3, L)),
            dma((3, S)),
            dma((3, S)),
        ],
        compiler_params=pltpu.CompilerParams(
            collective_id=0, has_side_effects=True, vmem_limit_bytes=48 * 1024 * 1024
        ),
    )(gap[0], stiffness[0], flexibility[0], packed)
    return (mult[None], res[None])


def solution(mesh):
    return jax.shard_map(
        per_device,
        mesh=mesh,
        in_specs=(
            P("sub", "ifc", None),
            P("sub", None, "ifc", None),
            P("sub", None, "ifc", None),
            P("sub", None, None, "ifc"),
            P("sub"),
        ),
        out_specs=(P("sub", "ifc", None), P("sub", "ifc", None)),
        check_vma=False,
    )
```

time: 289 us -> 65.9 us (0.23)
  blocking collectives: 207 us -> 0 us
  Pallas kernels: 0 us -> 58.9 us
  waiting for transfers between devices: 27.4 us -> 0 us
  matrix products: 19.6 us -> 0 us
  other arithmetic: 10.7 us -> 0.16 us
  local copies, waits for them, and re-layouts: 15 us -> 5.19 us
  starting transfers between devices: 6.67 us -> 0 us
    all_gather x6 -> x0, blocking collectives: 170 us -> none  [the longest x3 113 us: project(): lax.all_gather(partial_terms[None], ('sub', 'ifc'), axis=0, tiled=True)]
    pallas_call x0 -> x1, Pallas kernels: none -> 58.9 us  [per_device(): pl.pallas_call(functools.partial(kernel, S, L, R), out_shape=[jax.ShapeDt...]
    psum x1 -> x0, blocking collectives: 36.9 us -> none  [inner(): return lax.psum(jnp.sum(first_vec * second_vec, axis=0), ('sub', 'ifc'))]
    ppermute x5 -> x0, waiting for transfers between devices: 27.4 us -> none  [shifted_2(): return lax.ppermute(block, axis, route)]
    dot_general x17 -> x0, matrix products: 18.5 us -> none  [the longest x2 12.4 us: apply_jump(): image = jnp.einsum('aibj,bjk->aik', block_rows, traces, precision=precise)]
    another operation x2 -> x0, local copies, waits for them, and re-layouts: 13.2 us -> none  [apply_jump(): block_rows = matrix[0].reshape(2, own_rows, 2, face_len)]
    another operation x12 -> x0, other arithmetic: 9.5 us -> none  [the longest x3 5.05 us: per_device(): jnp.linalg.cholesky(assemble(gathered[:, 0], gathered[:, 1], gathered[:,...]
    ppermute x5 -> x0, starting transfers between devices: 6.67 us -> none  [shifted_2(): return lax.ppermute(block, axis, route)]
  transfers between devices with their start and end apart: 5 -> 0, of which waited for: 5 -> 0; matrix products, arithmetic and copies ran while one was open for 5% -> 0% of each run, Pallas kernels for 0% -> 0%
where the time goes in v1:
time: 65.9 us; the launch traced here: 65.6 us
  Pallas kernels  58.9 us (89%)
  local copies, waits for them, and re-layouts  5.19 us (8%)
  between operations  1.31 us (2%)
    pallas_call x1, Pallas kernels, per_device(): pl.pallas_call(functools.partial(kernel, S, L, R), out_shape=[jax.ShapeDt...  58.9 us
    unnamed x7, local copies, waits for them, and re-layouts  5.11 us

profile of v1, /device:TPU:0, one launch (start us, length us, event | category | flops | bytes accessed | tf_op | source)
XLA Modules:
  0.0 65.6 jit_solution(13911748234090984472)
XLA Ops:
  1.3 0.1 pad.7.clone
  1.4 0.7 %copy.9 = f32[1,6,2,256]{3,1,2,0:T(8,128)S(1)} copy(f32[1,6,2,256]{3,2,1,0:T(2,128)} %param.8) | data formatting | bytes 24576 | tf_op args[3]
  2.1 0.1 pad_multiply_fusion
  2.2 0.1 maximum_maximum_fusion.modes_ref
  2.2 0.0 copy-start
  2.2 2.2 %copy-done = f32[1,2,256,2048]{3,2,1,0:T(8,128)S(1)} copy-done((f32[1,2,256,2048]{3,2,1,0:T(8,128)S(1)}, f32[1,2,256,2048]{3,2,1,0:T(8,128)}, u32[]{:S(2)}) %copy-start) | copy-done | bytes 4194328
  4.4 0.0 copy-start.1
  4.4 0.9 %copy-done.1 = f32[1,256,128]{2,1,0:T(8,128)S(1)} copy-done((f32[1,256,128]{2,1,0:T(8,128)S(1)}, f32[1,256,128]{2,1,0:T(8,128)}, u32[]{:S(2)}) %copy-start.1) | copy-done | bytes 131096
  5.3 58.9 %shard_map.68 = (f32[256,128]{1,0:T(8,128)S(1)}, f32[256,128]{1,0:T(8,128)S(1)}) custom-call(f32[256,128]{1,0:T(8,128)S(1)} %bitcast.18, f32[2,256,2048]{2,1,0:T(8,128)S(1)} %bitcast.17, f32[2,256,2048]{2,1,0:T(8,128)} %bitcast.21, f32[24,256]{1,0:T(8,128)S(1)} %maximum_maximum_fusion.modes_ref), custom_call_target="tpu_custom_call" | custom-call | tf_op jit(solution)/shard_map/pallas_call | solution.py:338
  64.3 0.7 %copy.13 = f32[1,256,128]{2,1,0:T(8,128)} copy(f32[1,256,128]{2,1,0:T(8,128)S(1)} %bitcast.20) | data formatting | bytes 262144
  65.0 0.7 copy.14
  (3 shorter events, 0.0 us)
Async XLA Ops:
  2.2 2.2 %copy-start = (f32[1,2,256,2048]{3,2,1,0:T(8,128)S(1)}, f32[1,2,256,2048]{3,2,1,0:T(8,128)}, u32[]{:S(2)}) copy-start(f32[1,2,256,2048]{3,2,1,0:T(8,128)} %param.7) | copy-start | bytes 12582916
  4.4 0.9 %copy-start.1 = (f32[1,256,128]{2,1,0:T(8,128)S(1)}, f32[1,256,128]{2,1,0:T(8,128)}, u32[]{:S(2)}) copy-start(f32[1,256,128]{2,1,0:T(8,128)} %param.5) | copy-start | bytes 393220

commit v2 on v1

--- a/solution.py
+++ b/solution.py
@@ -30,8 +30,24 @@
     return hi, lo
 
 
+def thirds(a):
+    hi = a.astype(jnp.bfloat16).astype(f32)
+    mid = (a - hi).astype(jnp.bfloat16).astype(f32)
+    lo = (a - hi - mid).astype(jnp.bfloat16).astype(f32)
+    return hi, mid, lo
+
+
+def rows_times(a, b):
+    count, width = a.shape[0], b.shape[1]
+    hi = a.astype(jnp.bfloat16).astype(f32)
+    tall = jnp.concatenate([hi, a - hi], 0).astype(jnp.bfloat16)
+    wide = jnp.dot(tall, jnp.concatenate(split(b), 1), preferred_element_type=f32)
+    wide = wide[:count] + wide[count:]
+    return wide[:, :width] + wide[:, width:]
+
+
 def kernel(S, L, R, gap_ref, k_hbm, f_hbm, modes_ref, mult_ref, res_ref,
-           k_v, f_v, nbm, mt, t_buf, nbg, u_buf, nbu, v_buf, nbv, part, red, wbuf, own, acc,
+           k_v, f_v, nbm, mt, t_buf, nbg, u_buf, nbu, v_buf, nbv, part, red, wbuf, own, acc, mt_t, acc2,
            load_sem, nb_send, nb_recv, ag_send, ag_recv, mt_send, mt_recv,
            ln_send, ln_recv, sb_send, sb_recv):
     X = L // 2
@@ -190,7 +206,7 @@
     mt[lane, 0] = mt_l
     mt[lane, 1] = mt_r
     gram = dot_nt(mt_l[8:16], mt_l) + dot_nt(mt_r[8:16], mt_r)
-    part[0, lane, 0:24] = dot_nn(mt_r, t_buf[0, 1, lane])
+    part[0, lane, 0:24] = rows_times(mt_r, t_buf[0, 1, lane])
     part[0, lane, 24:32] = jnp.concatenate([gram, jnp.zeros((8, 104), f32)], 1)
     lane_send(0, 32)
     for d in range(1, L):
@@ -206,6 +222,13 @@
         modes_ref[16:24, 0:128], 0.0)
     sub_send(0, 32, jnp.concatenate([total[0:24], total[24:32] + idle], 0))
     ag_forward(0, 1)
+    for d in range(1, L):
+        src = lax.rem(lane + d, L)
+        rc(mt.at[src], mt.at[src], mt_send.at[d], mt_recv.at[src], s, src).wait_recv()
+    for j in range(L):
+        for f in range(2):
+            hi, mid, lo = thirds(mt[j, f])
+            mt_t[j, f] = jnp.transpose(jnp.concatenate([hi, hi, mid, hi, mid, lo], 0)).astype(jnp.bfloat16)
     sub_wait(0, 32)
 
     rows = []
@@ -218,54 +241,56 @@
     row_at = lax.broadcasted_iota(jnp.int32, (n, nw), 0)
     col_at = lax.broadcasted_iota(jnp.int32, (n, nw), 1)
 
-    def sweep(a, k, row):
-        col = jnp.sum(jnp.where(col_at == k, a, 0.0), axis=1, keepdims=True)
-        pivot = jnp.sum(jnp.where(col_at[0:1] == k, row, 0.0), axis=1, keepdims=True)
-        scale = 1.0 / pivot
-        scaled = jnp.where(col_at[0:1] == k, -scale, row * scale)
-        base = jnp.where(col_at == k, 0.0, a)
-        col = jnp.where(row_at[:, 0:1] == k, -1.0, col)
-        return jnp.where(row_at == k, scaled, base - col * jnp.where(col_at[0:1] == k, -scale, row * scale))
+    def sweep(a, k, row, col):
+        col = jnp.broadcast_to(col, (n, nw))
+        scale = 1.0 / jnp.sum(jnp.where(row_at == k, col, 0.0), axis=0, keepdims=True) if n > 64 else 1.0 / col[k:k + 1]
+        here = col_at == k
+        scaled = jnp.where(here[0:1], -scale, row * scale)
+        return jnp.where(row_at == k, scaled, jnp.where(here, 0.0, a) - col * scaled)
 
     if n <= 64:
         for t in range(S):
             for m in range(6):
                 k = 8 * t + m
-                coarse = sweep(coarse, k, coarse[k:k + 1])
+                coarse = sweep(coarse, k, coarse[k:k + 1], coarse[:, k:k + 1])
     else:
         def step(i, a):
             k = 8 * (i // 6) + lax.rem(i, 6)
-            return sweep(a, k, jnp.sum(jnp.where(row_at == k, a, 0.0), axis=0, keepdims=True))
+            return sweep(a, k, jnp.sum(jnp.where(row_at == k, a, 0.0), axis=0, keepdims=True),
+                         jnp.sum(jnp.where(col_at == k, a, 0.0), axis=1, keepdims=True))
         coarse = lax.fori_loop(0, 6 * S, step, coarse)
     pad = lax.rem(row_at, 8) >= 6
     inverse = jnp.where(pad, jnp.where(row_at == col_at, 1.0, 0.0), -coarse)[:, 0:n]
 
     ag_forward(0, 0)
-    for d in range(1, L):
-        src = lax.rem(lane + d, L)
-        rc(mt.at[src], mt.at[src], mt_send.at[d], mt_recv.at[src], s, src).wait_recv()
 
     def multiply(r, matrix, weights):
-        acc[...] = jnp.zeros_like(acc)
+        hi, mid, lo = thirds(weights)
+        stacked = jnp.concatenate([hi, mid, hi, lo, mid, hi], 0).astype(jnp.bfloat16)
         order = [(lane, False), (mate, True)]
         order += [(lax.rem(x + d, X) * 2 + core, False) for d in range(1, X)]
         order += [(lax.rem(x + d, X) * 2 + 1 - core, True) for d in range(1, X)]
-        for j, wait in order:
+        for at, (j, wait) in enumerate(order):
+            faces, his, los = [], [], []
             for f in (1, 0):
                 if wait:
                     ag_copy(r, f, j, 0, mate).wait_recv()
-                piece = t_buf[r, f, j] - dot_tn(mt[j, f], weights)
-                if j is lane:
+                piece = t_buf[r, f, j] - jnp.dot(mt_t[j, f], stacked, preferred_element_type=f32)
+                if at == 0:
                     own[r, f] = piece
+                faces.append(jnp.concatenate(split(piece), 1))
                 columns = pl.ds(pl.multiple_of(f * (L * R) + j * R, R), R)
-                p_hi, p_lo = split(piece)
-                for h in range(2):
-                    m_hi, m_lo = split(matrix[h, :, columns])
-                    acc[h] += (
-                        jnp.dot(m_hi, p_hi, preferred_element_type=f32)
-                        + jnp.dot(m_hi, p_lo, preferred_element_type=f32)
-                        + jnp.dot(m_lo, p_hi, preferred_element_type=f32)
-                    )
+                m_hi, m_lo = split(matrix[:, :, columns].reshape(2 * R, R))
+                his.append(m_hi)
+                los.append(m_lo)
+            wide = jnp.dot(jnp.concatenate(his + los, 1), jnp.concatenate(faces + faces, 0),
+                           preferred_element_type=f32)
+            if at == 0:
+                acc2[...] = wide
+            else:
+                acc2[...] += wide
+        acc[0] = acc2[0:R, 0:128] + acc2[0:R, 128:256]
+        acc[1] = acc2[R:2 * R, 0:128] + acc2[R:2 * R, 128:256]
 
     weights = weights_of(0, inverse)
     loads[0].wait()
@@ -276,7 +301,7 @@
     nb_start(3)
     nb_start(4)
     dots = jnp.sum(own[0, 0] * u_buf[0] + own[0, 1] * u_buf[1], axis=0, keepdims=True)
-    part[1, lane, 0:24] = dot_nn(mt_l, u_buf[0]) + dot_nn(mt_r, u_buf[1])
+    part[1, lane, 0:24] = rows_times(mt_l, u_buf[0]) + rows_times(mt_r, u_buf[1])
     part[1, lane, 24:32] = jnp.broadcast_to(dots, (8, 128))
     lane_send(1, 32)
     nb_wait(3)
@@ -296,7 +321,7 @@
     v_buf[...] = acc[0]
     nb_start(5)
     dots = jnp.sum(own[1, 0] * acc[0] + own[1, 1] * acc[1], axis=0, keepdims=True)
-    part[2, lane, 0:24] = dot_nn(mt_l, acc[0]) + dot_nn(mt_r, acc[1])
+    part[2, lane, 0:24] = rows_times(mt_l, acc[0]) + rows_times(mt_r, acc[1])
     part[2, lane, 24:32] = jnp.broadcast_to(dots, (8, 128))
     lane_send(2, 32)
     sub_send(2, 32, lane_sum(2, 32))
@@ -356,6 +381,8 @@
             pltpu.VMEM((3, n + 16, 128), f32),
             pltpu.VMEM((2, 2, R, loads), f32),
             pltpu.VMEM((2, R, loads), f32),
+            pltpu.VMEM((L, 2, R, 144), jnp.bfloat16),
+            pltpu.VMEM((2 * R, 2 * loads), f32),
             dma((2,)),
             dma((6,)),
             dma((6,)),
@@ -369,7 +396,7 @@
             dma((3, S)),
         ],
         compiler_params=pltpu.CompilerParams(
-            collective_id=0, has_side_effects=True, vmem_limit_bytes=48 * 1024 * 1024
+            collective_id=0, has_side_effects=True, vmem_limit_bytes=60 * 1024 * 1024
         ),
     )(gap[0], stiffness[0], flexibility[0], packed)
     return (mult[None], res[None])

time: 65.9 us -> 60.6 us (0.920)
  Pallas kernels: 58.9 us -> 54.4 us
  local copies, waits for them, and re-layouts: 5.19 us -> 3.92 us
    pallas_call x1, Pallas kernels: 58.9 us -> 54.4 us  [per_device(): pl.pallas_call(functools.partial(kernel, S, L, R), out_shape=[jax.ShapeDt...]
    unnamed x7 -> x3, local copies, waits for them, and re-layouts: 5.11 us -> 3.84 us
where the time goes in v2:
time: 60.6 us; the launch traced here: 60.4 us
  Pallas kernels  54.4 us (90%)
  local copies, waits for them, and re-layouts  3.92 us (6%)
  between operations  1.31 us (2%)
  other arithmetic  0.77 us (1%)
    pallas_call x1, Pallas kernels, per_device(): pl.pallas_call(functools.partial(kernel, S, L, R), out_shape=[jax.ShapeDt...  54.4 us
    unnamed x3, local copies, waits for them, and re-layouts  3.84 us

profile of v2, /device:TPU:0, one launch (start us, length us, event | category | flops | bytes accessed | tf_op | source)
XLA Modules:
  0.0 60.4 jit_solution(8950159468514320274)
XLA Ops:
  1.3 0.1 pad.7.clone
  1.4 0.7 %copy.9 = f32[1,6,2,256]{3,1,2,0:T(8,128)S(1)} copy(f32[1,6,2,256]{3,2,1,0:T(2,128)} %param.8) | data formatting | bytes 24576 | tf_op args[3]
  2.1 0.1 pad_multiply_fusion
  2.2 0.7 %maximum_maximum_fusion.modes_ref = f32[24,256]{1,0:T(8,128)} fusion(f32[8,256]{1,0:T(8,128)S(1)} %get-tuple-element.7, f32[8,256]{1,0:T(8,128)S(1)} %get-tuple-element.6, f32[24]{0:T(128)S(1)} %pad.7.clone), kind=kLoop, calls=%fused_computation | loop fusion | flops 12288 | bytes 41056 | tf_op jit(solution)/shard_map/concatenate | solution.py:359
  2.9 54.4 %shard_map.68 = (f32[256,128]{1,0:T(8,128)}, f32[256,128]{1,0:T(8,128)}) custom-call(f32[256,128]{1,0:T(8,128)} %bitcast.19, f32[2,256,2048]{2,1,0:T(8,128)} %bitcast.17, f32[2,256,2048]{2,1,0:T(8,128)} %bitcast.18, f32[24,256]{1,0:T(8,128)} %maximum_maximum_fusion.modes_ref), custom_call_target="tpu_custom_call" | custom-call | tf_op jit(solution)/shard_map/pallas_call | solution.py:363
  57.3 1.6 %copy.13 = f32[1,256,128]{2,1,0:T(8,128)} copy(f32[1,256,128]{2,1,0:T(8,128)} %bitcast.21) | data formatting | bytes 262144
  58.8 1.6 %copy.14 = f32[1,256,128]{2,1,0:T(8,128)} copy(f32[1,256,128]{2,1,0:T(8,128)} %bitcast.20) | data formatting | bytes 262144
  (3 shorter events, 0.0 us)

commit v3 on v2

--- a/solution.py
+++ b/solution.py
@@ -176,15 +176,15 @@
             row = red[r, t, 8:16]
             if t > 0:
                 row = row + red[r, t - 1, 16:24]
-            if t < S - 1:
+            if t < S - 1 and r > 0:
                 row = row + red[r, t + 1, 0:8]
-            rows.append(row)
+            rows.append(jnp.where(lax.broadcasted_iota(jnp.int32, (8, 128), 0) < 6, row, 0.0))
         return jnp.concatenate(rows, 0)
 
     def inner_of(r):
-        total = red[r, 0, 24:25]
+        total = red[r, 0, 14:15]
         for t in range(1, S):
-            total = total + red[r, t, 24:25]
+            total = total + red[r, t, 14:15]
         return total
 
     def weights_of(r, inverse):
@@ -206,9 +206,9 @@
     mt[lane, 0] = mt_l
     mt[lane, 1] = mt_r
     gram = dot_nt(mt_l[8:16], mt_l) + dot_nt(mt_r[8:16], mt_r)
-    part[0, lane, 0:24] = rows_times(mt_r, t_buf[0, 1, lane])
-    part[0, lane, 24:32] = jnp.concatenate([gram, jnp.zeros((8, 104), f32)], 1)
-    lane_send(0, 32)
+    part[0, lane, 8:24] = rows_times(mt_r, t_buf[0, 1, lane])[8:24]
+    part[0, lane, 0:8] = jnp.concatenate([gram, jnp.zeros((8, 104), f32)], 1)
+    lane_send(0, 24)
     for d in range(1, L):
         copy = rc(mt.at[lane], mt.at[lane], mt_send.at[d], mt_recv.at[lane], s, lax.rem(lane + d, L))
         copy.start()
@@ -216,11 +216,11 @@
     nb_wait(2)
     t_buf[0, 0, lane] = -nbg[...]
     ag_start(0, 0)
-    total = lane_sum(0, 32)
+    total = lane_sum(0, 24)
     idle = jnp.where(
         lax.broadcasted_iota(jnp.int32, (8, 128), 0) + 8 == lax.broadcasted_iota(jnp.int32, (8, 128), 1),
         modes_ref[16:24, 0:128], 0.0)
-    sub_send(0, 32, jnp.concatenate([total[0:24], total[24:32] + idle], 0))
+    sub_send(0, 24, jnp.concatenate([total[0:8] + idle, total[8:24]], 0))
     ag_forward(0, 1)
     for d in range(1, L):
         src = lax.rem(lane + d, L)
@@ -229,14 +229,15 @@
         for f in range(2):
             hi, mid, lo = thirds(mt[j, f])
             mt_t[j, f] = jnp.transpose(jnp.concatenate([hi, hi, mid, hi, mid, lo], 0)).astype(jnp.bfloat16)
-    sub_wait(0, 32)
+    sub_wait(0, 24)
 
     rows = []
     for t in range(S):
-        row = red[0, t, 24:32]
+        row = red[0, t, 0:8]
         if nw > 128:
             row = jnp.concatenate([row, jnp.zeros((8, nw - 128), f32)], 1)
         rows.append(pltpu.roll(row, (8 * (t - 1)) % nw, 1) if t != 1 else row)
+    blocks = rows
     coarse = jnp.concatenate(rows, 0)
     row_at = lax.broadcasted_iota(jnp.int32, (n, nw), 0)
     col_at = lax.broadcasted_iota(jnp.int32, (n, nw), 1)
@@ -249,10 +250,29 @@
         return jnp.where(row_at == k, scaled, jnp.where(here, 0.0, a) - col * scaled)
 
     if n <= 64:
-        for t in range(S):
+        couples = [[abs(i - j) <= 1 for j in range(S)] for i in range(S)]
+        row8, col8 = row_at[0:8], col_at[0:8]
+        remaining = list(range(S))
+        while remaining:
+            chosen, remaining = remaining[0::2], remaining[1::2]
             for m in range(6):
-                k = 8 * t + m
-                coarse = sweep(coarse, k, coarse[k:k + 1], coarse[:, k:k + 1])
+                fresh = list(blocks)
+                for t in chosen:
+                    k = 8 * t + m
+                    cols = {i: jnp.broadcast_to(blocks[i][:, k:k + 1], (8, nw)) for i in range(S) if couples[t][i]}
+                    scale = 1.0 / cols[t][m:m + 1]
+                    here = col8 == k
+                    scaled = jnp.where(here[0:1], -scale, blocks[t][m:m + 1] * scale)
+                    for i, col in cols.items():
+                        fresh[i] = jnp.where(here, 0.0, fresh[i]) - col * scaled
+                    fresh[t] = jnp.where(row8 == m, scaled, fresh[t])
+                blocks = fresh
+            for t in chosen:
+                near = [i for i in range(S) if couples[t][i]]
+                for i in near:
+                    for j in near:
+                        couples[i][j] = True
+        coarse = jnp.concatenate(blocks, 0)
     else:
         def step(i, a):
             k = 8 * (i // 6) + lax.rem(i, 6)
@@ -302,18 +322,18 @@
     nb_start(4)
     dots = jnp.sum(own[0, 0] * u_buf[0] + own[0, 1] * u_buf[1], axis=0, keepdims=True)
     part[1, lane, 0:24] = rows_times(mt_l, u_buf[0]) + rows_times(mt_r, u_buf[1])
-    part[1, lane, 24:32] = jnp.broadcast_to(dots, (8, 128))
-    lane_send(1, 32)
+    part[1, lane, 14:15] = dots
+    lane_send(1, 24)
     nb_wait(3)
     t_buf[1, 1, lane] = (u_buf[1] - nbu[1]) * m_r
     ag_start(1, 1)
     nb_wait(4)
     t_buf[1, 0, lane] = (u_buf[0] - nbu[0]) * m_l
     ag_start(1, 0)
-    sub_send(1, 32, lane_sum(1, 32))
+    sub_send(1, 24, lane_sum(1, 24))
     ag_forward(1, 1)
     ag_forward(1, 0)
-    sub_wait(1, 32)
+    sub_wait(1, 24)
     weights = weights_of(1, inverse)
     loads[1].wait()
     multiply(1, f_v, weights)
@@ -322,12 +342,12 @@
     nb_start(5)
     dots = jnp.sum(own[1, 0] * acc[0] + own[1, 1] * acc[1], axis=0, keepdims=True)
     part[2, lane, 0:24] = rows_times(mt_l, acc[0]) + rows_times(mt_r, acc[1])
-    part[2, lane, 24:32] = jnp.broadcast_to(dots, (8, 128))
-    lane_send(2, 32)
-    sub_send(2, 32, lane_sum(2, 32))
+    part[2, lane, 14:15] = dots
+    lane_send(2, 24)
+    sub_send(2, 24, lane_sum(2, 24))
     nb_wait(5)
     image = (acc[1] - nbv[...]) * m_r
-    sub_wait(2, 32)
+    sub_wait(2, 24)
     step_size = inner_of(1) / inner_of(2)
     image = image - dot_tn(mt_r, weights_of(2, inverse))
     mult_ref[...] = step_size * own[1, 1]
@@ -376,8 +396,8 @@
             pltpu.VMEM((2, R, loads), f32),
             pltpu.VMEM((R, loads), f32),
             pltpu.VMEM((R, loads), f32),
-            pltpu.VMEM((3, L, 32, 128), f32),
-            pltpu.VMEM((3, S, 32, 128), f32),
+            pltpu.VMEM((3, L, 24, 128), f32),
+            pltpu.VMEM((3, S, 24, 128), f32),
             pltpu.VMEM((3, n + 16, 128), f32),
             pltpu.VMEM((2, 2, R, loads), f32),
             pltpu.VMEM((2, R, loads), f32),

time: 60.6 us -> 57.3 us (0.946)
  Pallas kernels: 54.4 us -> 51.1 us
    pallas_call x1, Pallas kernels: 54.4 us -> 51.1 us  [per_device(): pl.pallas_call(functools.partial(kernel, S, L, R), out_shape=[jax.ShapeDt...]
where the time goes in v3:
time: 57.3 us; the launch traced here: 57.1 us
  Pallas kernels  51.1 us (89%)
  local copies, waits for them, and re-layouts  3.92 us (7%)
  between operations  1.31 us (2%)
  other arithmetic  0.77 us (1%)
    pallas_call x1, Pallas kernels, per_device(): pl.pallas_call(functools.partial(kernel, S, L, R), out_shape=[jax.ShapeDt...  51.1 us
    unnamed x3, local copies, waits for them, and re-layouts  3.84 us

profile of v3, /device:TPU:0, one launch (start us, length us, event | category | flops | bytes accessed | tf_op | source)
XLA Modules:
  0.0 57.1 jit_solution(7152329011084429364)
XLA Ops:
  1.3 0.1 pad.7.clone
  1.4 0.7 %copy.9 = f32[1,6,2,256]{3,1,2,0:T(8,128)S(1)} copy(f32[1,6,2,256]{3,2,1,0:T(2,128)} %param.8) | data formatting | bytes 24576 | tf_op args[3]
  2.1 0.1 pad_multiply_fusion
  2.2 0.7 %maximum_maximum_fusion.modes_ref = f32[24,256]{1,0:T(8,128)} fusion(f32[8,256]{1,0:T(8,128)S(1)} %get-tuple-element.7, f32[8,256]{1,0:T(8,128)S(1)} %get-tuple-element.6, f32[24]{0:T(128)S(1)} %pad.7.clone), kind=kLoop, calls=%fused_computation | loop fusion | flops 12288 | bytes 41056 | tf_op jit(solution)/shard_map/concatenate | solution.py:379
  2.9 51.1 %shard_map.68 = (f32[256,128]{1,0:T(8,128)}, f32[256,128]{1,0:T(8,128)}) custom-call(f32[256,128]{1,0:T(8,128)} %bitcast.19, f32[2,256,2048]{2,1,0:T(8,128)} %bitcast.17, f32[2,256,2048]{2,1,0:T(8,128)} %bitcast.18, f32[24,256]{1,0:T(8,128)} %maximum_maximum_fusion.modes_ref), custom_call_target="tpu_custom_call" | custom-call | tf_op jit(solution)/shard_map/pallas_call | solution.py:383
  54.0 1.6 %copy.13 = f32[1,256,128]{2,1,0:T(8,128)} copy(f32[1,256,128]{2,1,0:T(8,128)} %bitcast.21) | data formatting | bytes 262144
  55.5 1.6 %copy.14 = f32[1,256,128]{2,1,0:T(8,128)} copy(f32[1,256,128]{2,1,0:T(8,128)} %bitcast.20) | data formatting | bytes 262144
  (3 shorter events, 0.0 us)

commit v4 on v3

--- a/solution.py
+++ b/solution.py
@@ -195,7 +195,6 @@
 
     nb_start(0)
     nb_start(1)
-    ag_start(0, 1)
     nb_start(2)
     nb_wait(0)
     nb_wait(1)
@@ -213,6 +212,7 @@
         copy = rc(mt.at[lane], mt.at[lane], mt_send.at[d], mt_recv.at[lane], s, lax.rem(lane + d, L))
         copy.start()
         sends.append(copy)
+    ag_start(0, 1)
     nb_wait(2)
     t_buf[0, 0, lane] = -nbg[...]
     ag_start(0, 0)
@@ -416,7 +416,7 @@
             dma((3, S)),
         ],
         compiler_params=pltpu.CompilerParams(
-            collective_id=0, has_side_effects=True, vmem_limit_bytes=60 * 1024 * 1024
+            collective_id=0, has_side_effects=True, vmem_limit_bytes=52 * 1024 * 1024
         ),
     )(gap[0], stiffness[0], flexibility[0], packed)
     return (mult[None], res[None])

time: 57.3 us -> 54.4 us (0.949)
  Pallas kernels: 51.1 us -> 49.7 us
  local copies, waits for them, and re-layouts: 3.92 us -> 3 us
  other arithmetic: 0.77 us -> 0.16 us
    pallas_call x1, Pallas kernels: 51.1 us -> 49.7 us  [per_device(): pl.pallas_call(functools.partial(kernel, S, L, R), out_shape=[jax.ShapeDt...]
    unnamed x3 -> x5, local copies, waits for them, and re-layouts: 3.84 us -> 2.93 us
    concatenate x1, other arithmetic: 0.68 us -> 0.07 us  [per_device(): packed = jnp.concatenate([faces[0], faces[1] * live, idle], 0)]
where the time goes in v4:
time: 54.4 us; the launch traced here: 54.1 us
  Pallas kernels  49.7 us (91%)
  local copies, waits for them, and re-layouts  3 us (6%)
  between operations  1.31 us (2%)
    pallas_call x1, Pallas kernels, per_device(): pl.pallas_call(functools.partial(kernel, S, L, R), out_shape=[jax.ShapeDt...  49.7 us
    unnamed x5, local copies, waits for them, and re-layouts  2.93 us

profile of v4, /device:TPU:0, one launch (start us, length us, event | category | flops | bytes accessed | tf_op | source)
XLA Modules:
  0.0 54.1 jit_solution(9687729496896461392)
XLA Ops:
  1.3 0.1 pad.7.clone
  1.4 0.7 %copy.9 = f32[1,6,2,256]{3,1,2,0:T(8,128)S(1)} copy(f32[1,6,2,256]{3,2,1,0:T(2,128)} %param.8) | data formatting | bytes 24576 | tf_op args[3]
  2.1 0.1 pad_multiply_fusion
  2.2 0.1 maximum_maximum_fusion.modes_ref
  2.2 0.0 copy-start
  2.2 0.9 %copy-done = f32[1,256,128]{2,1,0:T(8,128)S(1)} copy-done((f32[1,256,128]{2,1,0:T(8,128)S(1)}, f32[1,256,128]{2,1,0:T(8,128)}, u32[]{:S(2)}) %copy-start) | copy-done | bytes 131096
  3.2 49.7 %shard_map.68 = (f32[256,128]{1,0:T(8,128)S(1)}, f32[256,128]{1,0:T(8,128)S(1)}) custom-call(f32[256,128]{1,0:T(8,128)S(1)} %bitcast.17, f32[2,256,2048]{2,1,0:T(8,128)} %bitcast.20, f32[2,256,2048]{2,1,0:T(8,128)} %bitcast.21, f32[24,256]{1,0:T(8,128)S(1)} %maximum_maximum_fusion.modes_ref), custom_call_target="tpu_custom_call" | custom-call | tf_op jit(solution)/shard_map/pallas_call | solution.py:383
  52.8 0.7 %copy.13 = f32[1,256,128]{2,1,0:T(8,128)} copy(f32[1,256,128]{2,1,0:T(8,128)S(1)} %bitcast.19) | data formatting | bytes 262144
  53.5 0.7 %copy.14 = f32[1,256,128]{2,1,0:T(8,128)} copy(f32[1,256,128]{2,1,0:T(8,128)S(1)} %bitcast.18) | data formatting | bytes 262144
  (3 shorter events, 0.0 us)
Async XLA Ops:
  2.2 0.9 %copy-start = (f32[1,256,128]{2,1,0:T(8,128)S(1)}, f32[1,256,128]{2,1,0:T(8,128)}, u32[]{:S(2)}) copy-start(f32[1,256,128]{2,1,0:T(8,128)} %param.5) | copy-start | bytes 393220
